TPU v7x, 32 devices: a whole 2x2x4 slice. The times are simulated.
32 devices in a mesh: spec: 16 (over z, x, core), img: 2 (over y).
Axes of the slice: x: 2, y: 2, z: 4, core: 2. Of those that a mesh axis runs over, the one named last changes fastest.
Arguments:
- spec_emb: bfloat16 [2048, 1024], P('spec', 'img'), may hold values from -1024 to 1024
- img_emb: bfloat16 [512, 1024], P('img', 'spec'), may hold values from -16 to 16
- grad_spec: bfloat16 [2048, 1024], P('spec', 'img'), may hold values from -6 to 6
- grad_img: bfloat16 [512, 1024], P('img', 'spec'), may hold values from -6 to 6
Outputs:
- spec_emb_grad: bfloat16 [2048, 1024], P('spec', 'img')
- img_emb_grad: bfloat16 [512, 1024], P('img', 'spec')
All inputs are finite; a program needn't handle non-finite values.
Results may differ from a plain program's by a relative error of at most 0.0109.
Values may be sent and summed in bfloat16 or wider, within the bound.
A program may use at most 64 MiB of HBM per device.

v0:
```python
import jax
import jax.numpy as jnp
from jax import lax
from jax.sharding import PartitionSpec as P

D = 1024
HEADS = 16
GROUP = 4


def row_totals(scores, moment):
    highest = lax.pmax(jnp.max(scores, axis=2, keepdims=True), "img")
    scaled = jnp.exp(scores - highest)
    total = lax.psum(jnp.sum(scaled, axis=2, keepdims=True), "img")
    weights = scaled / total
    delta = lax.psum(jnp.sum(weights * moment, axis=2, keepdims=True), "img")
    return (weights, delta)


def column_totals(scores, moment):
    highest = lax.pmax(jnp.max(scores, axis=1, keepdims=True), "spec")
    scaled = jnp.exp(scores - highest)
    total = lax.psum(jnp.sum(scaled, axis=1, keepdims=True), "spec")
    weights = scaled / total
    delta = lax.psum(jnp.sum(weights * moment, axis=1, keepdims=True), "spec")
    return (weights, delta)


def score_block(spec_rows, spec_grad, image_rows, image_grad, row_rule, column_rule):
    scale = (D // HEADS) ** (-0.5)
    scores = (
        jnp.einsum("shd,ihd->hsi", spec_rows, image_rows, preferred_element_type=jnp.float32)
        * scale
    )
    row_moment = jnp.einsum(
        "shd,ihd->hsi", spec_grad, image_rows, preferred_element_type=jnp.float32
    )
    column_moment = jnp.einsum(
        "shd,ihd->hsi", spec_rows, image_grad, preferred_element_type=jnp.float32
    )
    row_weight, row_delta = row_rule(scores, row_moment)
    column_weight, column_delta = column_rule(scores, column_moment)
    slope = (
        row_weight * (row_moment - row_delta) + column_weight * (column_moment - column_delta)
    ).astype(jnp.bfloat16)
    spec_part = scale * jnp.einsum(
        "hsi,ihd->shd", slope, image_rows, preferred_element_type=jnp.float32
    )
    spec_part = spec_part + jnp.einsum(
        "hsi,ihd->shd",
        column_weight.astype(jnp.bfloat16),
        image_grad,
        preferred_element_type=jnp.float32,
    )
    image_part = scale * jnp.einsum(
        "hsi,shd->ihd", slope, spec_rows, preferred_element_type=jnp.float32
    )
    image_part = image_part + jnp.einsum(
        "hsi,shd->ihd",
        row_weight.astype(jnp.bfloat16),
        spec_grad,
        preferred_element_type=jnp.float32,
    )
    return (spec_part, image_part)


def shards(spec_emb, img_emb, grad_spec, grad_img):
    head_size = D // HEADS
    spec_count = spec_emb.shape[0]
    spec_all, spec_grad_all = (
        lax.all_gather(spec_emb, "img", axis=1, tiled=True),
        lax.all_gather(grad_spec, "img", axis=1, tiled=True),
    )
    image_all, image_grad_all = (
        lax.all_gather(img_emb, "spec", axis=1, tiled=True),
        lax.all_gather(grad_img, "spec", axis=1, tiled=True),
    )
    image_count = image_all.shape[0]
    spec_heads = spec_all.reshape(spec_count, HEADS, head_size)
    spec_grad_heads = spec_grad_all.reshape(spec_count, HEADS, head_size)
    image_heads = image_all.reshape(image_count, HEADS, head_size)
    image_grad_heads = image_grad_all.reshape(image_count, HEADS, head_size)
    spec_parts = []
    image_parts = []
    for block_index in range(HEADS // GROUP):
        window = slice(block_index * GROUP, (block_index + 1) * GROUP)
        spec_part, image_part = score_block(
            spec_heads[:, window],
            spec_grad_heads[:, window],
            image_heads[:, window],
            image_grad_heads[:, window],
            row_totals,
            column_totals,
        )
        spec_parts.append(spec_part)
        image_parts.append(image_part)
    spec_total = jnp.concatenate(spec_parts, axis=1).reshape(spec_count, D)
    image_total = jnp.concatenate(image_parts, axis=1).reshape(image_count, D)
    spec_result = lax.psum_scatter(
        spec_total.astype(jnp.bfloat16), "img", scatter_dimension=1, tiled=True
    )
    image_result = lax.psum_scatter(image_total, "spec", scatter_dimension=1, tiled=True).astype(
        jnp.bfloat16
    )
    return (spec_result, image_result)


def solution(mesh):
    in_specs = (P("spec", "img"), P("img", "spec"), P("spec", "img"), P("img", "spec"))
    out_specs = (P("spec", "img"), P("img", "spec"))
    return jax.shard_map(shards, mesh=mesh, in_specs=in_specs, out_specs=out_specs, check_vma=False)
```

profile of v0, /device:TPU:0, one launch (start us, length us, event | category | flops | bytes accessed | tf_op | source)
XLA Modules:
  0.0 349.6 jit_solution(375095400356630244)
XLA Ops:
  7.2 7.4 %all_gather.12 = bf16[128,1024]{1,0:T(8,128)(2,1)S(1)} all-gather(bf16[128,512]{1,0:T(8,128)(2,1)} %param.4), channel_id=1, replica_groups=mesh['spec'=16,'img'=2] {'img'}, dimensions={1}, use_global_device_ids=true | all-gather | bytes 393216 | tf_op jit(solution)/shard_map/all_gather | solution.py:71
  14.8 0.6 copy-done.16
  15.4 23.4 %all_gather.15 = bf16[256,1024]{0,1:T(8,128)(2,1)S(1)} all-gather(bf16[256,64]{0,1:T(8,128)(2,1)S(1)} %copy-done.16), channel_id=1, replica_groups=mesh['spec'=16,'img'=2] {'spec'}, dimensions={1}, use_global_device_ids=true | all-gather | bytes 557056 | tf_op jit(solution)/shard_map/all_gather | solution.py:76
  38.8 1.1 fusion.37
  39.8 1.1 fusion.40
  40.9 0.3 fusion.43
  41.2 1.1 fusion.46
  42.3 18.9 %all_gather.13 = bf16[256,1024]{0,1:T(8,128)(2,1)S(1)} all-gather(bf16[256,64]{0,1:T(8,128)(2,1)S(1)} %copy-done.17), channel_id=1, replica_groups=mesh['spec'=16,'img'=2] {'spec'}, dimensions={1}, use_global_device_ids=true | all-gather | bytes 557056 | tf_op jit(solution)/shard_map/all_gather | solution.py:75
  61.1 0.4 fusion.83
  61.5 0.4 fusion.82
  61.8 0.4 fusion.81
  62.2 0.4 fusion.80
  62.6 0.5 copy-done.15
  63.1 6.5 %all_gather.14 = bf16[128,1024]{1,0:T(8,128)(2,1)} all-gather(bf16[128,512]{1,0:T(8,128)(2,1)S(1)} %copy-done.15), channel_id=1, replica_groups=mesh['spec'=16,'img'=2] {'img'}, dimensions={1}, use_global_device_ids=true | all-gather | bytes 393216 | tf_op jit(solution)/shard_map/all_gather | solution.py:72
  69.6 1.8 copy.7
  71.4 5.0 %all-reduce.5 = (f32[4,128]{1,0:T(4,128)S(1)}, f32[4,128]{1,0:T(4,128)S(1)}, f32[4,128]{1,0:T(4,128)S(1)}, f32[4,128]{1,0:T(4,128)S(1)}) all-reduce(f32[4,128]{1,0:T(4,128)S(1)} %get-tuple-element.24, f32[4,128]{1,0:T(4,128)S(1)} %get-tuple-element.18, ...), channel_id=1, replica_groups=mesh['spec'=16,'img'=2] {'img'}, use_global_device_ids=true, to_apply=%region_37.0 | all-reduce | flops 2048 | bytes 16384 | tf_op jit(solution)/shard_map/pmax | solution.py:12
  76.4 57.6 %all-reduce.2 = (f32[4,256]{1,0:T(4,128)S(1)}, f32[4,256]{1,0:T(4,128)S(1)}, f32[4,256]{1,0:T(4,128)S(1)}, f32[4,256]{1,0:T(4,128)S(1)}) all-reduce(f32[4,256]{1,0:T(4,128)S(1)} %get-tuple-element.25, f32[4,256]{1,0:T(4,128)S(1)} %get-tuple-element.19, ...), channel_id=1, replica_groups=mesh['spec'=16,'img'=2] {'spec'}, use_global_device_ids=true, to_apply=%region_43.0 | all-reduce | flops 4096 | bytes 32768 | tf_op jit(solution)/shard_map/pmax | solution.py:21
  134.0 0.3 fusion.25
  134.3 0.3 fusion.21
  134.6 0.3 fusion.17
  134.8 0.3 fusion.13
  135.1 5.0 %all-reduce.4 = (f32[4,128]{1,0:T(4,128)S(1)}, f32[4,128]{1,0:T(4,128)S(1)}, f32[4,128]{1,0:T(4,128)S(1)}, f32[4,128]{1,0:T(4,128)S(1)}) all-reduce(f32[4,128]{1,0:T(4,128)S(1)} %get-tuple-element.22, f32[4,128]{1,0:T(4,128)S(1)} %get-tuple-element.16, ...), channel_id=1, replica_groups=mesh['spec'=16,'img'=2] {'img'}, use_global_device_ids=true, to_apply=%region_39.0 | all-reduce | flops 2048 | bytes 16384 | tf_op jit(solution)/shard_map/psum | solution.py:14
  140.1 57.6 %all-reduce.1 = (f32[4,256]{1,0:T(4,128)S(1)}, f32[4,256]{1,0:T(4,128)S(1)}, f32[4,256]{1,0:T(4,128)S(1)}, f32[4,256]{1,0:T(4,128)S(1)}) all-reduce(f32[4,256]{1,0:T(4,128)S(1)} %get-tuple-element.23, f32[4,256]{1,0:T(4,128)S(1)} %get-tuple-element.17, ...), channel_id=1, replica_groups=mesh['spec'=16,'img'=2] {'spec'}, use_global_device_ids=true, to_apply=%region_45.0 | all-reduce | flops 4096 | bytes 32768 | tf_op jit(solution)/shard_map/psum | solution.py:23
  197.7 2.3 multiply_reduce_fusion.1
  200.0 1.1 multiply_reduce_fusion.3
  201.1 1.1 multiply_reduce_fusion.5
  202.3 1.1 multiply_reduce_fusion.7
  203.4 5.0 %all-reduce.3 = (f32[4,128]{1,0:T(4,128)S(1)}, f32[4,128]{1,0:T(4,128)S(1)}, f32[4,128]{1,0:T(4,128)S(1)}, f32[4,128]{1,0:T(4,128)S(1)}) all-reduce(f32[4,128]{1,0:T(4,128)S(1)} %get-tuple-element.20, f32[4,128]{1,0:T(4,128)S(1)} %get-tuple-element.14, ...), channel_id=1, replica_groups=mesh['spec'=16,'img'=2] {'img'}, use_global_device_ids=true, to_apply=%region_41.0 | all-reduce | flops 2048 | bytes 16384 | tf_op jit(solution)/shard_map/psum | solution.py:16
  208.4 57.6 %all-reduce = (f32[4,256]{1,0:T(4,128)S(1)}, f32[4,256]{1,0:T(4,128)S(1)}, f32[4,256]{1,0:T(4,128)S(1)}, f32[4,256]{1,0:T(4,128)S(1)}) all-reduce(f32[4,256]{1,0:T(4,128)S(1)} %get-tuple-element.21, f32[4,256]{1,0:T(4,128)S(1)} %get-tuple-element.15, f32[4,256]{1,0:T(4,128)S(1)} %get-tuple-element.9, ...), channel_id=1, replica_groups=mesh['spec'=16,'img'=2] {'spec'}, use_global_device_ids=true, to_apply=%region_47.0 | all-reduce | flops 4096 | bytes 32768 | tf_op jit(solution)/shard_map/psum | solution.py:25
  266.0 1.8 add_convert_fusion
  268.1 0.8 copy-done.14
  268.8 0.4 fusion
  269.4 0.4 fusion.1
  269.8 0.6 copy-done.7
  270.9 0.6 add_convert_fusion.2
  271.8 0.5 copy-done
  272.3 0.4 fusion.3
  272.8 0.4 fusion.2
  273.2 1.1 pad_maximum_fusion
  274.8 0.7 copy-done.3
  275.7 0.7 copy-done.1
  276.7 0.2 fusion.8
  276.9 0.2 fusion.9
  277.1 0.2 fusion.11
  277.7 0.9 copy.8
  278.5 50.6 %reduce-scatter.5.cloned.1.call-done = f32[256,64]{0,1:T(8,128)} async-done(((f32[256,1024]{0,1:T(8,128)}), f32[256,64]{0,1:T(8,128)}) %reduce-scatter.5.cloned.1.call-update) | async-done | bytes 65552 | tf_op jit(solution)/shard_map/reduce_scatter | solution.py:102
  329.2 1.5 convert_element_type.56
  330.6 12.1 %reduce-scatter.3.cloned.1.call-done = bf16[128,512]{1,0:T(8,128)(2,1)} async-done(((bf16[128,1024]{1,0:T(8,128)(2,1)}), bf16[128,512]{1,0:T(8,128)(2,1)}) %reduce-scatter.3.cloned.1.call-update) | async-done | bytes 131088 | tf_op jit(solution)/shard_map/reduce_scatter | solution.py:99
  (44 shorter events, 2.6 us)
Async XLA Ops:
  7.2 322.0 %reduce-scatter.5.cloned.1.call-start = ((), (), s32[]{:S(2)}) async-start(), calls=%async_computation.3 | async-start | bytes 1114112 | tf_op jit(solution)/shard_map/reduce_scatter | solution.py:102
  14.6 0.8 copy-start.16
  38.8 2.4 copy-start.4
  41.2 159.9 %copy-start.6 = (f32[4,128,256]{2,1,0:T(8,128)}, f32[4,128,256]{2,1,0:T(8,128)S(1)}, u32[]{:S(2)}) copy-start(f32[4,128,256]{2,1,0:T(8,128)S(1)} %fusion.43) | copy-start | bytes 1572868
  41.2 1.1 copy-start.17
  62.2 0.9 copy-start.15
  197.7 2.3 copy-start.10
  197.7 2.3 copy-start.13
  201.1 1.1 copy-start.8
  267.9 1.0 copy-start.14
  269.4 1.0 copy-start.7
  269.4 1.2 copy-start.9
  269.4 1.3 copy-start.11
  269.4 1.5 copy-start.12
  271.6 0.7 copy-start
  271.6 1.1 copy-start.2
  274.3 68.5 %reduce-scatter.3.cloned.1.call-start = ((), (), s32[]{:S(2)}) async-start(), calls=%async_computation.2 | async-start | bytes 393216 | tf_op jit(solution)/shard_map/reduce_scatter | solution.py:99
  274.5 1.0 copy-start.3
  275.5 0.9 copy-start.1
  275.5 1.2 copy-start.5
Sparse Core Ops, SparseCore 0:
  274.4 54.7 reduce-scatter.4
  332.0 10.6 reduce-scatter.2
where the time goes:
time: 350 us
  blocking collectives  244 us (70%)
  waiting for transfers between devices  62.8 us (18%)
  matrix products  14.5 us (4%)
  between operations  14.3 us (4%)
  local copies, waits for them, and re-layouts  7.86 us (2%)
  other arithmetic  6.09 us (2%)
    pmax x1, blocking collectives, column_totals(): highest = lax.pmax(jnp.max(scores, axis=1, keepdims=True), 'spec')  57.6 us
    psum x1, blocking collectives, column_totals(): total = lax.psum(jnp.sum(scaled, axis=1, keepdims=True), 'spec')  57.6 us
    psum x1, blocking collectives, column_totals(): delta = lax.psum(jnp.sum(weights * moment, axis=1, keepdims=True), 'spec')  57.6 us
    reduce_scatter x1, waiting for transfers between devices, shards(): lax.psum_scatter(image_total, 'spec', scatter_dimension=1, tiled=True)  50.6 us
    all_gather x1, blocking collectives, shards(): lax.all_gather(grad_img, 'spec', axis=1, tiled=True)  23.4 us
    all_gather x1, blocking collectives, shards(): lax.all_gather(img_emb, 'spec', axis=1, tiled=True)  18.9 us
    reduce_scatter x1, waiting for transfers between devices, shards(): lax.psum_scatter(spec_total.astype(jnp.bfloat16), 'img', scatter_dimensio...  12.1 us
    all_gather x1, blocking collectives, shards(): lax.all_gather(spec_emb, 'img', axis=1, tiled=True)  7.39 us
  transfers between devices with their start and end apart: 2, of which 2 were waited for; matrix products, arithmetic and copies ran while one was open for 1% of the time, Pallas kernels for 0%

commit v1 on v0

--- a/solution.py
+++ b/solution.py
@@ -1,6 +1,10 @@
+import functools
+
 import jax
 import jax.numpy as jnp
 from jax import lax
+from jax.experimental import pallas as pl
+from jax.experimental.pallas import tpu as pltpu
 from jax.sharding import PartitionSpec as P
 
 D = 1024
@@ -105,7 +109,292 @@
     return (spec_result, image_result)
 
 
+F32 = jnp.float32
+BF16 = jnp.bfloat16
+NT = (((1,), (1,)), ((), ()))
+TN = (((0,), (0,)), ((), ()))
+NN = (((1,), (0,)), ((), ()))
+
+
+def dot(a, b, dims):
+    return lax.dot_general(a, b, dims, preferred_element_type=F32)
+
+
+def head_kernel(
+    chips, scale,
+    spec_emb, img_emb, grad_spec, grad_img, spec_out, img_out,
+    x_send, x, y_send, y, w, z, p, q, s16, c16, acc,
+    stat_send, stat, part, part_in, o_send, o, g_send, g,
+    xs_sem, xr_sem, ys_sem, yr_sem, os_sem, or_sem, pair_send, pair_recv, gs_sem, gr_sem,
+):
+    rows = spec_emb.shape[0]
+    half = rows // 2
+    size = img_emb.shape[1]
+    cols = y.shape[1]
+    images = 2 * cols
+    me_s, me_i = lax.axis_index("spec"), lax.axis_index("img")
+    chip, core = me_s // 2, me_s % 2
+    mine = me_i * chips + chip
+    to_s, to_i = 2 * (me_s % chips), me_s // chips
+    is_self = (to_s + me_i == me_s) & (to_i == me_i)
+
+    def remote(src, dst, send, recv, s, i):
+        return pltpu.make_async_remote_copy(
+            src_ref=src, dst_ref=dst, send_sem=send, recv_sem=recv,
+            device_id={"spec": s, "img": i}, device_id_type=pl.DeviceIdType.MESH,
+        )
+
+    barrier = pltpu.get_barrier_semaphore()
+
+    def greet(s, i):
+        pl.semaphore_signal(
+            barrier, inc=1, device_id={"spec": s, "img": i}, device_id_type=pl.DeviceIdType.MESH
+        )
+
+    for t in range(1, chips):
+        greet(2 * lax.rem(chip + t, chips) + core, me_i)
+    sibling = 2 * chip + 1 - core
+    greet(sibling, me_i)
+    for i in range(2):
+        own = (mine == me_s) & (me_i == i)
+
+        @pl.when(jnp.logical_not(own))
+        def _():
+            greet(mine, i)
+
+    @pl.when(jnp.logical_not(is_self))
+    def _():
+        greet(to_s + me_i, to_i)
+
+    y_send[...] = jnp.concatenate([img_emb[...], grad_img[...]], axis=1)
+    for j in range(chips):
+        part_of = slice(j * size, (j + 1) * size)
+        x_send[j] = jnp.concatenate([spec_emb[:, part_of], grad_spec[:, part_of]], axis=1)
+
+    @pl.when(is_self)
+    def _():
+        pl.semaphore_wait(barrier, chips + 1)
+
+    @pl.when(jnp.logical_not(is_self))
+    def _():
+        pl.semaphore_wait(barrier, chips + 3)
+
+    def image_copy(cc):
+        return remote(y_send, y.at[me_i], ys_sem.at[cc], yr_sem.at[me_i], to_s + cc, to_i)
+
+    for cc in range(2):
+        own = (to_s + cc == me_s) & (to_i == me_i)
+
+        @pl.when(jnp.logical_not(own))
+        def _():
+            image_copy(cc).start()
+
+        @pl.when(own)
+        def _():
+            y[me_i] = y_send[...]
+
+    def x_copy(j):
+        return remote(
+            x_send.at[j], x.at[chip], xs_sem.at[j], xr_sem.at[chip], 2 * j + core, me_i
+        )
+
+    for t in range(1, chips):
+        x_copy(lax.rem(chip + t, chips)).start()
+    x[chip] = x_send[chip]
+
+    for i in range(2):
+        own = (mine == me_s) & (me_i == i)
+
+        @pl.when(jnp.logical_not(own))
+        def _():
+            remote(y_send, y.at[i], ys_sem.at[0], yr_sem.at[i], mine, i).wait_recv()
+
+        both = y[i]
+        e, d = both[:, :size], both[:, size:]
+        zero = jnp.zeros_like(e)
+        w[pl.ds(i * cols, cols)] = jnp.concatenate([e, zero], axis=1)
+        w[pl.ds(images + i * cols, cols)] = jnp.concatenate([zero, e], axis=1)
+        w[pl.ds(2 * images + i * cols, cols)] = jnp.concatenate([d, zero], axis=1)
+
+    def arrive(t, carry):
+        top, total, moment = carry
+        j = lax.rem(chip + chips - t, chips)
+
+        @pl.when(t > 0)
+        def _():
+            remote(
+                x_send.at[j], x.at[j], xs_sem.at[j], xr_sem.at[j], 2 * j + core, me_i
+            ).wait_recv()
+
+        all3 = dot(x[j], w[...], NT)
+        zj = all3[:, :images] * scale
+        qj = all3[:, 2 * images :]
+        z[j] = zj
+        p[j] = all3[:, images : 2 * images]
+        q[j] = qj
+        new = jnp.maximum(top, jnp.max(zj, axis=0, keepdims=True))
+        fade = jnp.exp(top - new)
+        e = jnp.exp(zj - new)
+        total = total * fade + jnp.sum(e, axis=0, keepdims=True)
+        moment = moment * fade + jnp.sum(e * qj, axis=0, keepdims=True)
+        return new, total, moment
+
+    start = jnp.full((1, images), -jnp.inf, F32)
+    nothing = jnp.zeros((1, images), F32)
+    top, total, moment = lax.fori_loop(0, chips, arrive, (start, nothing, nothing))
+    stat_send[0:1] = top
+    stat_send[1:2] = total
+    stat_send[2:3] = moment
+    stat_copy = remote(stat_send, stat, pair_send.at[0], pair_recv.at[0], sibling, me_i)
+    stat_copy.start()
+
+    acc[...] = jnp.zeros_like(acc)
+
+    def by_row(j, carry):
+        zj, pj = z[j], p[j]
+        e = jnp.exp(zj - jnp.max(zj, axis=1, keepdims=True))
+        weight = e * (1.0 / jnp.sum(e, axis=1, keepdims=True))
+        delta = jnp.sum(weight * pj, axis=1, keepdims=True)
+        p[j] = weight * (pj - delta)
+        acc[...] += dot(x[j], weight.astype(BF16), TN)[size:]
+        return carry
+
+    lax.fori_loop(0, chips, by_row, 0)
+
+    stat_copy.wait()
+    other = stat[0:1]
+    high = jnp.maximum(top, other)
+    here, there = jnp.exp(top - high), jnp.exp(other - high)
+    inverse = 1.0 / (total * here + stat[1:2] * there)
+    column_delta = (moment * here + stat[2:3] * there) * inverse
+
+    def by_column(j, carry):
+        weight = jnp.exp(z[j] - high) * inverse
+        slope = (p[j] + weight * (q[j] - column_delta)).astype(BF16)
+        s16[j] = slope
+        c16[j] = weight.astype(BF16)
+        acc[...] += scale * dot(x[j], slope, TN)[:size]
+        return carry
+
+    lax.fori_loop(0, chips, by_column, 0)
+    for i in range(2):
+        part[i] = acc[:, i * cols : (i + 1) * cols]
+    part_copy = remote(part.at[1 - core], part_in, pair_send.at[1], pair_recv.at[1], sibling, me_i)
+    part_copy.start()
+
+    def o_copy(j):
+        return remote(
+            o_send.at[j], o.at[chip], os_sem.at[j], or_sem.at[chip], 2 * j + core, me_i
+        )
+
+    features = jnp.concatenate([y[0], y[1]], axis=0)
+
+    def spec_rows(t, carry):
+        j = lax.rem(chip + t, chips)
+        value = scale * dot(s16[j], features, NN)[:, :size] + dot(c16[j], features, NN)[:, size:]
+        o_send[j] = jnp.concatenate([value[:half], value[half:]], axis=1).astype(BF16)
+        o_copy(j).start()
+        return carry
+
+    lax.fori_loop(1, chips, spec_rows, 0)
+    part_copy.wait()
+    g_send[...] = (part[core] + part_in[...]).astype(BF16)
+    g_copy = remote(g_send, g, gs_sem, gr_sem, mine, core)
+
+    out_self = (mine == me_s) & (core == me_i)
+
+    @pl.when(jnp.logical_not(out_self))
+    def _():
+        g_copy.start()
+
+    @pl.when(out_self)
+    def _():
+        g[...] = g_send[...]
+
+    value = scale * dot(s16[chip], features, NN)[:, :size] + dot(c16[chip], features, NN)[:, size:]
+    o[chip] = jnp.concatenate([value[:half], value[half:]], axis=1).astype(BF16)
+
+    for t in range(1, chips):
+        j = lax.rem(chip + chips - t, chips)
+        remote(o_send.at[j], o.at[j], os_sem.at[j], or_sem.at[j], 2 * j + core, me_i).wait_recv()
+    for a in range(chips // 2):
+        b0, b1 = o[2 * a], o[2 * a + 1]
+        spec_out[:half, 2 * a * size : 2 * (a + 1) * size] = jnp.concatenate(
+            [b0[:, :size], b1[:, :size]], axis=1
+        )
+        spec_out[half:, 2 * a * size : 2 * (a + 1) * size] = jnp.concatenate(
+            [b0[:, size:], b1[:, size:]], axis=1
+        )
+
+    @pl.when(jnp.logical_not(is_self))
+    def _():
+        remote(g_send, g, gs_sem, gr_sem, to_s + me_i, to_i).wait_recv()
+
+    img_out[...] = g[...].astype(F32).T.astype(BF16)
+
+    for t in range(1, chips):
+        j = lax.rem(chip + t, chips)
+        x_copy(j).wait_send()
+        o_copy(j).wait_send()
+    for cc in range(2):
+        own = (to_s + cc == me_s) & (to_i == me_i)
+
+        @pl.when(jnp.logical_not(own))
+        def _():
+            image_copy(cc).wait_send()
+
+    @pl.when(jnp.logical_not(out_self))
+    def _():
+        g_copy.wait_send()
+
+
+def head_shards(chips, spec_emb, img_emb, grad_spec, grad_img):
+    rows, width = spec_emb.shape
+    cols, size = img_emb.shape
+    images = 2 * cols
+    vmem, dma = pltpu.VMEM, pltpu.SemaphoreType.DMA
+    return pl.pallas_call(
+        functools.partial(head_kernel, chips, size**-0.5),
+        out_shape=(
+            jax.ShapeDtypeStruct((rows, width), BF16),
+            jax.ShapeDtypeStruct((cols, size), BF16),
+        ),
+        in_specs=[pl.BlockSpec(memory_space=vmem)] * 4,
+        out_specs=[pl.BlockSpec(memory_space=vmem)] * 2,
+        scratch_shapes=[
+            vmem((chips, rows, 2 * size), BF16),
+            vmem((chips, rows, 2 * size), BF16),
+            vmem((cols, 2 * size), BF16),
+            vmem((2, cols, 2 * size), BF16),
+            vmem((3 * images, 2 * size), BF16),
+            vmem((chips, rows, images), F32),
+            vmem((chips, rows, images), F32),
+            vmem((chips, rows, images), F32),
+            vmem((chips, rows, images), BF16),
+            vmem((chips, rows, images), BF16),
+            vmem((size, images), F32),
+            vmem((8, images), F32),
+            vmem((8, images), F32),
+            vmem((2, size, cols), F32),
+            vmem((size, cols), F32),
+            vmem((chips, rows // 2, 2 * size), BF16),
+            vmem((chips, rows // 2, 2 * size), BF16),
+            vmem((size, cols), BF16),
+            vmem((size, cols), BF16),
+            dma((chips,)), dma((chips,)), dma((2,)), dma((2,)),
+            dma((chips,)), dma((chips,)), dma((2,)), dma((2,)), dma, dma,
+        ],
+        compiler_params=pltpu.CompilerParams(
+            collective_id=0, has_side_effects=True, vmem_limit_bytes=40 * 2**20
+        ),
+    )(spec_emb, img_emb, grad_spec, grad_img)
+
+
 def solution(mesh):
     in_specs = (P("spec", "img"), P("img", "spec"), P("spec", "img"), P("img", "spec"))
     out_specs = (P("spec", "img"), P("img", "spec"))
-    return jax.shard_map(shards, mesh=mesh, in_specs=in_specs, out_specs=out_specs, check_vma=False)
+    chips = mesh.shape["spec"] // 2
+    body = shards
+    if mesh.shape["spec"] == HEADS and mesh.shape["img"] == 2 and chips % 2 == 0:
+        body = functools.partial(head_shards, chips)
+    return jax.shard_map(body, mesh=mesh, in_specs=in_specs, out_specs=out_specs, check_vma=False)

time: 350 us -> 31.7 us (0.09)
  blocking collectives: 244 us -> 0 us
  waiting for transfers between devices: 62.8 us -> 0 us
  Pallas kernels: 0 us -> 27.6 us
  matrix products: 14.5 us -> 0 us
  between operations: 14.3 us -> 0.69 us
  other arithmetic: 6.09 us -> 0 us
  local copies, waits for them, and re-layouts: 7.86 us -> 3.29 us
    psum x4 -> x0, blocking collectives: 125 us -> none  [the longest x1 57.6 us: column_totals(): total = lax.psum(jnp.sum(scaled, axis=1, keepdims=True), 'spec')]
    reduce_scatter x2 -> x0, waiting for transfers between devices: 62.7 us -> none  [the longest x1 50.6 us: shards(): lax.psum_scatter(image_total, 'spec', scatter_dimension=1, tiled=True)]
    pmax x2 -> x0, blocking collectives: 62.6 us -> none  [the longest x1 57.6 us: column_totals(): highest = lax.pmax(jnp.max(scores, axis=1, keepdims=True), 'spec')]
    all_gather x4 -> x0, blocking collectives: 56.2 us -> none  [the longest x1 23.4 us: shards(): lax.all_gather(grad_img, 'spec', axis=1, tiled=True)]
    pallas_call x0 -> x1, Pallas kernels: none -> 27.6 us  [head_shards(): pl.pallas_call(functools.partial(head_kernel, chips, size ** (-0.5)), out...]
    dot_general x28 -> x0, matrix products: 14.5 us -> none  [the longest x4 5.69 us: score_block(): jnp.einsum('shd,ihd->hsi', spec_grad, image_rows, preferred_element_type=...]
    convert_element_type x3 -> x0, other arithmetic: 3.95 us -> none  [the longest x2 2.49 us: score_block(): slope = (row_weight * (row_moment - row_delta) + column_weight * (column_...]
  transfers between devices with their start and end apart: 2 -> 0, of which waited for: 2 -> 0; matrix products, arithmetic and copies ran while one was open for 1% -> 0% of each run, Pallas kernels for 0% -> 0%
where the time goes in v1:
time: 31.7 us; the launch traced here: 31.6 us
  Pallas kernels  27.6 us (87%)
  local copies, waits for them, and re-layouts  3.29 us (10%)
  between operations  0.69 us (2%)
    pallas_call x1, Pallas kernels, head_shards(): pl.pallas_call(functools.partial(head_kernel, chips, size ** (-0.5)), out...  27.6 us
    unnamed x9, local copies, waits for them, and re-layouts  2.58 us
    pallas_call x1, local copies, waits for them, and re-layouts, head_shards(): pl.pallas_call(functools.partial(head_kernel, chips, size ** (-0.5)), out...  0.71 us

profile of v1, /device:TPU:0, one launch (start us, length us, event | category | flops | bytes accessed | tf_op | source)
XLA Modules:
  0.0 31.6 jit_solution(1543315876321258023)
XLA Ops:
  0.6 0.0 copy-start.2
  0.6 0.0 copy-start
  0.6 0.9 %copy.6.img_emb = bf16[256,64]{1,0:T(8,128)(2,1)S(1)} copy(bf16[256,64]{0,1:T(8,128)(2,1)} %param.5) | data formatting | bytes 65536 | tf_op args[1]
  1.6 0.0 copy-done.2
  1.6 0.1 copy.7.grad_img
  1.7 0.0 copy-done
  1.7 0.0 copy-start.1
  1.7 0.9 %copy-done.1 = bf16[128,512]{1,0:T(8,128)(2,1)S(1)} copy-done((bf16[128,512]{1,0:T(8,128)(2,1)S(1)}, bf16[128,512]{1,0:T(8,128)(2,1)}, u32[]{:S(2)}) %copy-start.1) | copy-done | bytes 131096
  2.6 27.6 %shard_map.59 = (bf16[128,512]{1,0:T(8,128)(2,1)S(1)}, bf16[256,64]{1,0:T(8,128)(2,1)S(1)}) custom-call(bf16[128,512]{1,0:T(8,128)(2,1)S(1)} %copy-done, bf16[256,64]{1,0:T(8,128)(2,1)S(1)} %copy.6.img_emb, bf16[128,512]{1,0:T(8,128)(2,1)S(1)} %copy-done.1, bf16[256,64]{1,0:T(8,128)(2,1)S(1)} %copy.7.grad_img), custom_call_target="tpu_custom_call" | custom-call | tf_op jit(solution)/shard_map/pallas_call | solution.py:356
  30.2 0.7 %copy.8 = bf16[256,64]{0,1:T(8,128)(2,1)} copy(bf16[256,64]{1,0:T(8,128)(2,1)S(1)} %get-tuple-element.3) | data formatting | bytes 65536 | tf_op jit(solution)/shard_map/pallas_call | solution.py:356
  30.9 0.7 %copy.10 = bf16[128,512]{1,0:T(8,128)(2,1)} copy(bf16[128,512]{1,0:T(8,128)(2,1)S(1)} %get-tuple-element.6) | data formatting | bytes 262144
Async XLA Ops:
  0.6 0.9 %copy-start.2 = (bf16[256,64]{0,1:T(8,128)(2,1)S(1)}, bf16[256,64]{0,1:T(8,128)(2,1)}, u32[]{:S(2)}) copy-start(bf16[256,64]{0,1:T(8,128)(2,1)} %param.7) | copy-start | bytes 98308
  0.6 1.0 %copy-start = (bf16[128,512]{1,0:T(8,128)(2,1)S(1)}, bf16[128,512]{1,0:T(8,128)(2,1)}, u32[]{:S(2)}) copy-start(bf16[128,512]{1,0:T(8,128)(2,1)} %spec_emb.1) | copy-start | bytes 393220
  1.7 0.9 %copy-start.1 = (bf16[128,512]{1,0:T(8,128)(2,1)S(1)}, bf16[128,512]{1,0:T(8,128)(2,1)}, u32[]{:S(2)}) copy-start(bf16[128,512]{1,0:T(8,128)(2,1)} %grad_spec.1) | copy-start | bytes 393220

commit v2 on v1

--- a/solution.py
+++ b/solution.py
@@ -122,15 +122,15 @@
 
 def head_kernel(
     chips, scale,
-    spec_emb, img_emb, grad_spec, grad_img, spec_out, img_out,
-    x_send, x, y_send, y, w, z, p, q, s16, c16, acc,
+    spec_emb_in, img_emb_in, grad_spec_in, grad_img_in, spec_out, img_out,
+    x_send, x, y_send, y, w, z, p, q, acc,
     stat_send, stat, part, part_in, o_send, o, g_send, g,
     xs_sem, xr_sem, ys_sem, yr_sem, os_sem, or_sem, pair_send, pair_recv, gs_sem, gr_sem,
+    spec_emb, grad_spec, load_sem, features,
 ):
-    rows = spec_emb.shape[0]
+    rows = spec_emb_in.shape[0]
     half = rows // 2
-    size = img_emb.shape[1]
-    cols = y.shape[1]
+    size, cols = img_emb_in.shape
     images = 2 * cols
     me_s, me_i = lax.axis_index("spec"), lax.axis_index("img")
     chip, core = me_s // 2, me_s % 2
@@ -144,6 +144,17 @@
             device_id={"spec": s, "img": i}, device_id_type=pl.DeviceIdType.MESH,
         )
 
+    loads = [
+        pltpu.make_async_copy(src, dst, load_sem.at[n])
+        for n, (src, dst) in enumerate(
+            (
+                (img_emb_in, y_send.at[pl.ds(0, size)]),
+                (grad_img_in, y_send.at[pl.ds(size, size)]),
+                (spec_emb_in, spec_emb),
+                (grad_spec_in, grad_spec),
+            )
+        )
+    ]
     barrier = pltpu.get_barrier_semaphore()
 
     def greet(s, i):
@@ -166,7 +177,10 @@
     def _():
         greet(to_s + me_i, to_i)
 
-    y_send[...] = jnp.concatenate([img_emb[...], grad_img[...]], axis=1)
+    for load in loads:
+        load.start()
+    for load in loads:
+        load.wait()
     for j in range(chips):
         part_of = slice(j * size, (j + 1) * size)
         x_send[j] = jnp.concatenate([spec_emb[:, part_of], grad_spec[:, part_of]], axis=1)
@@ -209,14 +223,22 @@
         def _():
             remote(y_send, y.at[i], ys_sem.at[0], yr_sem.at[i], mine, i).wait_recv()
 
-        both = y[i]
-        e, d = both[:, :size], both[:, size:]
+        e, d = y[i, :size], y[i, size:]
         zero = jnp.zeros_like(e)
-        w[pl.ds(i * cols, cols)] = jnp.concatenate([e, zero], axis=1)
-        w[pl.ds(images + i * cols, cols)] = jnp.concatenate([zero, e], axis=1)
-        w[pl.ds(2 * images + i * cols, cols)] = jnp.concatenate([d, zero], axis=1)
-
-    def arrive(t, carry):
+        for n, pair in enumerate(((e, zero), (zero, e), (d, zero))):
+            w[:size, n * images + i * cols : n * images + (i + 1) * cols] = pair[0]
+            w[size:, n * images + i * cols : n * images + (i + 1) * cols] = pair[1]
+
+    acc[...] = jnp.zeros_like(acc)
+
+    def by_row(j, zj, pj):
+        e = jnp.exp(zj - jnp.max(zj, axis=1, keepdims=True))
+        weight = e * (1.0 / jnp.sum(e, axis=1, keepdims=True))
+        delta = jnp.sum(weight * pj, axis=1, keepdims=True)
+        p[j] = weight * (pj - delta)
+        acc[...] += dot(x[j], weight.astype(BF16), TN)[size:]
+
+    def arrive(with_rows, t, carry):
         top, total, moment = carry
         j = lax.rem(chip + chips - t, chips)
 
@@ -226,11 +248,15 @@
                 x_send.at[j], x.at[j], xs_sem.at[j], xr_sem.at[j], 2 * j + core, me_i
             ).wait_recv()
 
-        all3 = dot(x[j], w[...], NT)
+        all3 = dot(x[j], w[...], NN)
         zj = all3[:, :images] * scale
         qj = all3[:, 2 * images :]
         z[j] = zj
-        p[j] = all3[:, images : 2 * images]
+        pj = all3[:, images : 2 * images]
+        if with_rows:
+            by_row(j, zj, pj)
+        else:
+            p[j] = pj
         q[j] = qj
         new = jnp.maximum(top, jnp.max(zj, axis=0, keepdims=True))
         fade = jnp.exp(top - new)
@@ -241,26 +267,24 @@
 
     start = jnp.full((1, images), -jnp.inf, F32)
     nothing = jnp.zeros((1, images), F32)
-    top, total, moment = lax.fori_loop(0, chips, arrive, (start, nothing, nothing))
+    early = chips // 2
+    sums = lax.fori_loop(0, early, functools.partial(arrive, True), (start, nothing, nothing))
+    top, total, moment = lax.fori_loop(early, chips, functools.partial(arrive, False), sums)
     stat_send[0:1] = top
     stat_send[1:2] = total
     stat_send[2:3] = moment
     stat_copy = remote(stat_send, stat, pair_send.at[0], pair_recv.at[0], sibling, me_i)
     stat_copy.start()
 
-    acc[...] = jnp.zeros_like(acc)
-
-    def by_row(j, carry):
-        zj, pj = z[j], p[j]
-        e = jnp.exp(zj - jnp.max(zj, axis=1, keepdims=True))
-        weight = e * (1.0 / jnp.sum(e, axis=1, keepdims=True))
-        delta = jnp.sum(weight * pj, axis=1, keepdims=True)
-        p[j] = weight * (pj - delta)
-        acc[...] += dot(x[j], weight.astype(BF16), TN)[size:]
+    def late(t, carry):
+        j = lax.rem(chip + chips - t, chips)
+        by_row(j, z[j], p[j])
         return carry
 
-    lax.fori_loop(0, chips, by_row, 0)
-
+    lax.fori_loop(early, chips, late, 0, unroll=2)
+
+    for i in range(2):
+        features[pl.ds(i * cols, cols)] = y[i].T
     stat_copy.wait()
     other = stat[0:1]
     high = jnp.maximum(top, other)
@@ -268,35 +292,32 @@
     inverse = 1.0 / (total * here + stat[1:2] * there)
     column_delta = (moment * here + stat[2:3] * there) * inverse
 
-    def by_column(j, carry):
+    def o_copy(j):
+        return remote(
+            o_send.at[j], o.at[chip], os_sem.at[j], or_sem.at[chip], 2 * j + core, me_i
+        )
+
+    def by_column(t, carry):
+        j = lax.rem(chip + t, chips)
         weight = jnp.exp(z[j] - high) * inverse
         slope = (p[j] + weight * (q[j] - column_delta)).astype(BF16)
-        s16[j] = slope
-        c16[j] = weight.astype(BF16)
         acc[...] += scale * dot(x[j], slope, TN)[:size]
+        value = scale * dot(slope, features[...], NN)[:, :size]
+        value += dot(weight.astype(BF16), features[...], NN)[:, size:]
+        o_send[j] = jnp.concatenate([value[:half], value[half:]], axis=1).astype(BF16)
+
+        @pl.when(t < chips)
+        def _():
+            o_copy(j).start()
+
         return carry
 
-    lax.fori_loop(0, chips, by_column, 0)
+    lax.fori_loop(1, chips + 1, by_column, 0, unroll=2)
     for i in range(2):
         part[i] = acc[:, i * cols : (i + 1) * cols]
     part_copy = remote(part.at[1 - core], part_in, pair_send.at[1], pair_recv.at[1], sibling, me_i)
     part_copy.start()
 
-    def o_copy(j):
-        return remote(
-            o_send.at[j], o.at[chip], os_sem.at[j], or_sem.at[chip], 2 * j + core, me_i
-        )
-
-    features = jnp.concatenate([y[0], y[1]], axis=0)
-
-    def spec_rows(t, carry):
-        j = lax.rem(chip + t, chips)
-        value = scale * dot(s16[j], features, NN)[:, :size] + dot(c16[j], features, NN)[:, size:]
-        o_send[j] = jnp.concatenate([value[:half], value[half:]], axis=1).astype(BF16)
-        o_copy(j).start()
-        return carry
-
-    lax.fori_loop(1, chips, spec_rows, 0)
     part_copy.wait()
     g_send[...] = (part[core] + part_in[...]).astype(BF16)
     g_copy = remote(g_send, g, gs_sem, gr_sem, mine, core)
@@ -311,8 +332,7 @@
     def _():
         g[...] = g_send[...]
 
-    value = scale * dot(s16[chip], features, NN)[:, :size] + dot(c16[chip], features, NN)[:, size:]
-    o[chip] = jnp.concatenate([value[:half], value[half:]], axis=1).astype(BF16)
+    o[chip] = o_send[chip]
 
     for t in range(1, chips):
         j = lax.rem(chip + chips - t, chips)
@@ -330,7 +350,7 @@
     def _():
         remote(g_send, g, gs_sem, gr_sem, to_s + me_i, to_i).wait_recv()
 
-    img_out[...] = g[...].astype(F32).T.astype(BF16)
+    img_out[...] = g[...]
 
     for t in range(1, chips):
         j = lax.rem(chip + t, chips)
@@ -353,25 +373,23 @@
     cols, size = img_emb.shape
     images = 2 * cols
     vmem, dma = pltpu.VMEM, pltpu.SemaphoreType.DMA
-    return pl.pallas_call(
+    spec_grad, img_grad = pl.pallas_call(
         functools.partial(head_kernel, chips, size**-0.5),
         out_shape=(
             jax.ShapeDtypeStruct((rows, width), BF16),
-            jax.ShapeDtypeStruct((cols, size), BF16),
+            jax.ShapeDtypeStruct((size, cols), BF16),
         ),
-        in_specs=[pl.BlockSpec(memory_space=vmem)] * 4,
+        in_specs=[pl.BlockSpec(memory_space=pltpu.HBM)] * 4,
         out_specs=[pl.BlockSpec(memory_space=vmem)] * 2,
         scratch_shapes=[
             vmem((chips, rows, 2 * size), BF16),
             vmem((chips, rows, 2 * size), BF16),
-            vmem((cols, 2 * size), BF16),
-            vmem((2, cols, 2 * size), BF16),
-            vmem((3 * images, 2 * size), BF16),
+            vmem((2 * size, cols), BF16),
+            vmem((2, 2 * size, cols), BF16),
+            vmem((2 * size, 3 * images), BF16),
             vmem((chips, rows, images), F32),
             vmem((chips, rows, images), F32),
             vmem((chips, rows, images), F32),
-            vmem((chips, rows, images), BF16),
-            vmem((chips, rows, images), BF16),
             vmem((size, images), F32),
             vmem((8, images), F32),
             vmem((8, images), F32),
@@ -383,11 +401,14 @@
             vmem((size, cols), BF16),
             dma((chips,)), dma((chips,)), dma((2,)), dma((2,)),
             dma((chips,)), dma((chips,)), dma((2,)), dma((2,)), dma, dma,
+            vmem((rows, width), BF16), vmem((rows, width), BF16), dma((4,)),
+            vmem((images, 2 * size), BF16),
         ],
         compiler_params=pltpu.CompilerParams(
             collective_id=0, has_side_effects=True, vmem_limit_bytes=40 * 2**20
         ),
-    )(spec_emb, img_emb, grad_spec, grad_img)
+    )(spec_emb, img_emb.T, grad_spec, grad_img.T)
+    return spec_grad, img_grad.T
 
 
 def solution(mesh):

time: 31.7 us -> 30.8 us (0.972); the launches traced: 31.6 us -> 30.4 us
  Pallas kernels: 27.6 us -> 25.1 us
  local copies, waits for them, and re-layouts: 3.29 us -> 4.59 us
    pallas_call x1, Pallas kernels: 27.6 us -> 25.1 us  [head_shards(): pl.pallas_call(functools.partial(head_kernel, chips, size ** (-0.5)), out...]
    unnamed x9 -> x10, local copies, waits for them, and re-layouts: 2.58 us -> 4.59 us
    pallas_call x1 -> x0, local copies, waits for them, and re-layouts: 0.71 us -> none  [head_shards(): pl.pallas_call(functools.partial(head_kernel, chips, size ** (-0.5)), out...]
where the time goes in v2:
time: 30.8 us; the launch traced here: 30.4 us
  Pallas kernels  25.1 us (81%)
  local copies, waits for them, and re-layouts  4.59 us (15%)
  between operations  0.65 us (2%)
    pallas_call x1, Pallas kernels, head_shards(): pl.pallas_call(functools.partial(head_kernel, chips, size ** (-0.5)), out...  25.1 us
    unnamed x10, local copies, waits for them, and re-layouts  4.59 us

profile of v2, /device:TPU:0, one launch (start us, length us, event | category | flops | bytes accessed | tf_op | source)
XLA Modules:
  0.0 30.4 jit_solution(13004923842240748957)
XLA Ops:
  0.6 0.0 copy-start
  0.6 0.9 %copy-done = bf16[128,512]{1,0:T(8,128)(2,1)S(1)} copy-done((bf16[128,512]{1,0:T(8,128)(2,1)S(1)}, bf16[128,512]{1,0:T(8,128)(2,1)}, u32[]{:S(2)}) %copy-start) | copy-done | bytes 131096
  1.5 0.0 copy-start.1
  1.5 0.9 %copy-done.1 = bf16[128,512]{1,0:T(8,128)(2,1)S(1)} copy-done((bf16[128,512]{1,0:T(8,128)(2,1)S(1)}, bf16[128,512]{1,0:T(8,128)(2,1)}, u32[]{:S(2)}) %copy-start.1) | copy-done | bytes 131096
  2.4 0.0 copy-start.2
  2.4 0.8 %copy-done.2 = bf16[256,64]{0,1:T(8,128)(2,1)S(1)} copy-done((bf16[256,64]{0,1:T(8,128)(2,1)S(1)}, bf16[256,64]{0,1:T(8,128)(2,1)}, u32[]{:S(2)}) %copy-start.2) | copy-done | bytes 32792
  3.2 0.0 copy-start.3
  3.2 0.8 %copy-done.3 = bf16[256,64]{0,1:T(8,128)(2,1)S(1)} copy-done((bf16[256,64]{0,1:T(8,128)(2,1)S(1)}, bf16[256,64]{0,1:T(8,128)(2,1)}, u32[]{:S(2)}) %copy-start.3) | copy-done | bytes 32792
  4.0 25.1 %shard_map.59 = (bf16[128,512]{1,0:T(8,128)(2,1)S(1)}, bf16[64,256]{1,0:T(8,128)(2,1)S(1)}) custom-call(bf16[128,512]{1,0:T(8,128)(2,1)S(1)} %copy-done, bf16[64,256]{1,0:T(8,128)(2,1)S(1)} %bitcast.3, bf16[128,512]{1,0:T(8,128)(2,1)S(1)} %copy-done.1, bf16[64,256]{1,0:T(8,128)(2,1)S(1)} %bitcast.4), custom_call_target="tpu_custom_call" | custom-call | tf_op jit(solution)/shard_map/pallas_call | solution.py:376
  29.1 0.7 %copy.8 = bf16[128,512]{1,0:T(8,128)(2,1)} copy(bf16[128,512]{1,0:T(8,128)(2,1)S(1)} %get-tuple-element.8) | data formatting | bytes 262144
  29.7 0.6 %copy.9 = bf16[256,64]{0,1:T(8,128)(2,1)} copy(bf16[256,64]{0,1:T(8,128)(2,1)S(1)} %bitcast.5) | data formatting | bytes 65536
Async XLA Ops:
  0.6 0.9 %copy-start = (bf16[128,512]{1,0:T(8,128)(2,1)S(1)}, bf16[128,512]{1,0:T(8,128)(2,1)}, u32[]{:S(2)}) copy-start(bf16[128,512]{1,0:T(8,128)(2,1)} %spec_emb_in.1) | copy-start | bytes 393220
  1.5 0.9 %copy-start.1 = (bf16[128,512]{1,0:T(8,128)(2,1)S(1)}, bf16[128,512]{1,0:T(8,128)(2,1)}, u32[]{:S(2)}) copy-start(bf16[128,512]{1,0:T(8,128)(2,1)} %grad_spec_in.1) | copy-start | bytes 393220
  2.4 0.8 %copy-start.2 = (bf16[256,64]{0,1:T(8,128)(2,1)S(1)}, bf16[256,64]{0,1:T(8,128)(2,1)}, u32[]{:S(2)}) copy-start(bf16[256,64]{0,1:T(8,128)(2,1)} %param.5) | copy-start | bytes 98308
  3.2 0.8 %copy-start.3 = (bf16[256,64]{0,1:T(8,128)(2,1)S(1)}, bf16[256,64]{0,1:T(8,128)(2,1)}, u32[]{:S(2)}) copy-start(bf16[256,64]{0,1:T(8,128)(2,1)} %param.7) | copy-start | bytes 98308
